TPU v7x, 128 devices: a whole 4x4x4 slice. The times are simulated.
128 devices in a mesh: ctx: 32 (over z, x, core), head: 4 (over y).
Axes of the slice: x: 4, y: 4, z: 4, core: 2. Of those that a mesh axis runs over, the one named last changes fastest.
Arguments:
- queries: bfloat16 [16384, 8192], P(('ctx', 'head')), may hold values from -6 to 6
- key_states: bfloat16 [16384, 1024], P(('ctx', 'head')), may hold values from -6 to 6
- value_states: bfloat16 [16384, 1024], P(('ctx', 'head')), may hold values from -6 to 6
- out_grads: bfloat16 [16384, 8192], P(('ctx', 'head')), may hold values from -6 to 6
- doc_blocks: int32 [16], replicated, may hold values from 1 to 12, 128 in all
Outputs:
- attended: bfloat16 [16384, 8192], P('ctx', 'head')
- query_grads: bfloat16 [16384, 8192], P('ctx', 'head')
- key_grads: bfloat16 [16384, 1024], P('ctx', 'head')
- value_grads: bfloat16 [16384, 1024], P('ctx', 'head')
Inputs may be any that keep to these rules, and one draw needn't show every extreme that they name: `doc_blocks`: the lengths sum to 128; the longest is exactly 12.
All inputs are finite; a program needn't handle non-finite values.
Results may differ from a plain program's by a relative error of at most 0.012.
The roundings to bfloat16 on the way count: a program that leaves them out, or rounds other values in their place, can miss the bound.
Values may be sent and summed in bfloat16 or wider, within the bound.
A program may use at most 128 MiB of HBM per device.

v0:
```python
import math

import jax
import jax.numpy as jnp
from jax import lax
from jax.sharding import PartitionSpec as P

HQ = 64
HK = 8
DH = 128
BLOCK = 128
SPAN = 3
MAXDOC = 12


MASKED = -1e30


def from_behind(value, axis, steps):
    count = lax.axis_size(axis)
    first, last = (max(0, -steps), min(count, count - steps))
    return lax.ppermute(value, axis, [(source, source + steps) for source in range(first, last)])


def block_starts(doc_blocks, total_blocks):
    doc_ends = jnp.cumsum(doc_blocks)
    doc_begins = doc_ends - doc_blocks
    block_ids = jnp.arange(total_blocks, dtype=jnp.int32)
    inside = (block_ids[:, None] >= doc_begins[None, :]) & (block_ids[:, None] < doc_ends[None, :])
    return jnp.sum(jnp.where(inside, doc_begins[None, :], 0), axis=1)


def attend(
    query_blocks, grad_blocks, block_index, first_block, key_window, value_window, window_base
):
    block_len = query_blocks.shape[1]
    kv_heads = key_window.shape[2]
    head_size = key_window.shape[3]
    inv_root = 1.0 / math.sqrt(query_blocks.shape[-1])
    positions = jnp.arange(block_len, dtype=jnp.int32)
    causal = positions[None, :] <= positions[:, None]
    window_tiles = key_window.shape[0]
    span_tiles = min(MAXDOC, window_tiles)
    tile_ids = jnp.repeat(
        jnp.arange(span_tiles, dtype=jnp.int32),
        block_len,
        total_repeat_length=span_tiles * block_len,
    )
    key_pos = jnp.tile(positions, span_tiles)

    def tile_scores(query_block, target, source):
        slot_index = source - window_base
        key_tile = lax.dynamic_index_in_dim(key_window, slot_index, 0, keepdims=False)
        value_tile = lax.dynamic_index_in_dim(value_window, slot_index, 0, keepdims=False)
        scores = (
            jnp.einsum("qhgd,khd->hgqk", query_block, key_tile, preferred_element_type=jnp.float32)
            * inv_root
        )
        allowed = causal | (source < target)
        return (jnp.where(allowed, scores, MASKED), key_tile, value_tile, slot_index)

    def one_block(position, carried):
        outputs, query_grads, key_grads, value_grads = carried
        query_block = lax.dynamic_index_in_dim(query_blocks, position, 0, keepdims=False)
        grad_block = lax.dynamic_index_in_dim(grad_blocks, position, 0, keepdims=False)
        target = block_index[position]
        doc_start = first_block[target]
        tile_count = target - doc_start + 1
        slice_start = jnp.clip(target - span_tiles + 1 - window_base, 0, window_tiles - span_tiles)
        key_span = lax.dynamic_slice_in_dim(key_window, slice_start, span_tiles, 0).reshape(
            span_tiles * block_len, kv_heads, head_size
        )
        value_span = lax.dynamic_slice_in_dim(value_window, slice_start, span_tiles, 0).reshape(
            span_tiles * block_len, kv_heads, head_size
        )
        sources = window_base + slice_start + tile_ids
        allowed = (sources[None, :] >= doc_start) & (
            (sources[None, :] < target)
            | (sources[None, :] == target) & (key_pos[None, :] <= positions[:, None])
        )
        span_scores = (
            jnp.einsum("qhgd,khd->hgqk", query_block, key_span, preferred_element_type=jnp.float32)
            * inv_root
        )
        span_scores = jnp.where(allowed, span_scores, MASKED)
        row_top = jnp.max(span_scores, axis=-1)
        log_total = row_top + jnp.log(jnp.sum(jnp.exp(span_scores - row_top[..., None]), axis=-1))
        span_rounded = jnp.exp(span_scores - log_total[..., None]).astype(jnp.bfloat16)
        accumulated = jnp.einsum(
            "hgqk,khd->qhgd", span_rounded, value_span, preferred_element_type=jnp.float32
        )
        result = accumulated.astype(jnp.bfloat16)
        row_delta = jnp.transpose(
            jnp.sum(grad_block.astype(jnp.float32) * result.astype(jnp.float32), axis=-1), (1, 2, 0)
        )

        def backward(offset, grad_state):
            query_grad, key_grad_win, value_grad_win = grad_state
            scores, key_tile, value_tile, slot_index = tile_scores(
                query_block, target, doc_start + offset
            )
            weights = jnp.exp(scores - log_total[..., None])
            rounded = weights.astype(jnp.bfloat16)
            value_term = jnp.einsum(
                "hgqk,qhgd->khd", rounded, grad_block, preferred_element_type=jnp.float32
            )
            dweights = jnp.einsum(
                "qhgd,khd->hgqk", grad_block, value_tile, preferred_element_type=jnp.float32
            )
            dscores = (weights * (dweights - row_delta[..., None])).astype(jnp.bfloat16)
            query_grad = (
                query_grad
                + jnp.einsum(
                    "hgqk,khd->qhgd", dscores, key_tile, preferred_element_type=jnp.float32
                )
                * inv_root
            )
            key_term = (
                jnp.einsum(
                    "hgqk,qhgd->khd", dscores, query_block, preferred_element_type=jnp.float32
                )
                * inv_root
            )
            previous_key = lax.dynamic_index_in_dim(key_grad_win, slot_index, 0, keepdims=False)
            previous_value = lax.dynamic_index_in_dim(value_grad_win, slot_index, 0, keepdims=False)
            key_grad_win = lax.dynamic_update_index_in_dim(
                key_grad_win, previous_key + key_term, slot_index, 0
            )
            value_grad_win = lax.dynamic_update_index_in_dim(
                value_grad_win, previous_value + value_term, slot_index, 0
            )
            return (query_grad, key_grad_win, value_grad_win)

        query_grad, key_grads, value_grads = lax.fori_loop(
            0,
            tile_count,
            backward,
            (jnp.zeros(query_block.shape, jnp.float32), key_grads, value_grads),
        )
        outputs = lax.dynamic_update_index_in_dim(outputs, result, position, 0)
        query_grads = lax.dynamic_update_index_in_dim(
            query_grads, query_grad.astype(jnp.bfloat16), position, 0
        )
        return (outputs, query_grads, key_grads, value_grads)

    initial = (
        jnp.zeros(query_blocks.shape, jnp.bfloat16),
        jnp.zeros(query_blocks.shape, jnp.bfloat16),
        jnp.zeros(key_window.shape, jnp.float32),
        jnp.zeros(value_window.shape, jnp.float32),
    )
    return lax.fori_loop(0, query_blocks.shape[0], one_block, initial)


def shards(queries, key_states, value_states, out_grads, doc_blocks):
    local_q, local_k, local_v, local_g = (
        lax.all_to_all(queries, "head", split_axis=1, concat_axis=0, tiled=True),
        lax.all_to_all(key_states, "head", split_axis=1, concat_axis=0, tiled=True),
        lax.all_to_all(value_states, "head", split_axis=1, concat_axis=0, tiled=True),
        lax.all_to_all(out_grads, "head", split_axis=1, concat_axis=0, tiled=True),
    )
    tokens_here = local_q.shape[0]
    block_count = tokens_here // BLOCK
    kv_heads = local_k.shape[1] // DH
    group_size = HQ // HK
    query_blocks = local_q.reshape(block_count, BLOCK, kv_heads, group_size, DH)
    grad_blocks = local_g.reshape(block_count, BLOCK, kv_heads, group_size, DH)
    own_pair = jnp.stack(
        [
            local_k.reshape(block_count, BLOCK, kv_heads, DH),
            local_v.reshape(block_count, BLOCK, kv_heads, DH),
        ]
    )
    ctx_count = lax.axis_size("ctx")
    device = lax.axis_index("ctx")
    first_block = block_starts(doc_blocks, block_count * ctx_count)
    earlier = []
    for distance in range(SPAN, 0, -1):
        earlier.append(from_behind(own_pair, "ctx", distance))
    near_window = jnp.concatenate(earlier + [own_pair], axis=1)
    block_index = device * block_count + jnp.arange(block_count, dtype=jnp.int32)
    attended, query_grads, key_part, value_part = attend(
        query_blocks,
        grad_blocks,
        block_index,
        first_block,
        near_window[0],
        near_window[1],
        (device - SPAN) * block_count,
    )
    own_slot = SPAN
    kv_part = jnp.stack([key_part, value_part])
    kv_total = kv_part[:, own_slot * block_count : (own_slot + 1) * block_count]
    for distance in range(SPAN, 0, -1):
        slot_start = (own_slot - distance) * block_count
        kv_total = kv_total + from_behind(
            kv_part[:, slot_start : slot_start + block_count], "ctx", -distance
        )
    kv_final = kv_total.astype(jnp.bfloat16)
    return (
        attended.reshape(tokens_here, -1),
        query_grads.reshape(tokens_here, -1),
        kv_final[0].reshape(tokens_here, -1),
        kv_final[1].reshape(tokens_here, -1),
    )


def solution(mesh):
    placed = (
        P(("ctx", "head"), None),
        P(("ctx", "head"), None),
        P(("ctx", "head"), None),
        P(("ctx", "head"), None),
        P(),
    )
    return jax.shard_map(
        shards,
        mesh=mesh,
        in_specs=placed,
        out_specs=(P("ctx", "head"), P("ctx", "head"), P("ctx", "head"), P("ctx", "head")),
        check_vma=False,
    )
```

profile of v0, /device:TPU:41, one launch (start us, length us, event | category | flops | bytes accessed | tf_op | source)
XLA Modules:
  0.0 532.3 jit_solution(7755418392317755636)
XLA Ops:
  0.6 1.9 copy.47
  2.6 4.3 all-to-all-start
  6.9 1.8 copy.48
  8.7 2.6 all-to-all-done
  11.3 4.5 all-to-all-start.1
  15.9 2.4 copy.50
  18.3 1.9 all-to-all-done.1
  20.2 5.7 %all-to-all-start.2 = ((bf16[128,4,2048]{0,2,1:T(8,128)(2,1)}), bf16[128,4,2048]{0,2,1:T(8,128)(2,1)}, u32[]{:S(2)}, u32[]{:S(2)}) async-start(bf16[128,4,2048]{0,2,1:T(8,128)(2,1)} %bitcast.29), calls=%async_computation.2 | async-start | bytes 4194304 | tf_op jit(solution)/shard_map/all_to_all | solution.py:157
  25.9 2.4 copy.70
  28.3 19.6 %all-to-all-done.2 = bf16[128,4,2048]{0,2,1:T(8,128)(2,1)} async-done(((bf16[128,4,2048]{0,2,1:T(8,128)(2,1)}), bf16[128,4,2048]{0,2,1:T(8,128)(2,1)}, u32[]{:S(2)}, u32[]{:S(2)}) %all-to-all-start.2) | async-done | bytes 2097184 | tf_op jit(solution)/shard_map/all_to_all | solution.py:157
  48.0 5.7 %all-to-all-start.3 = ((bf16[128,4,2048]{0,2,1:T(8,128)(2,1)}), bf16[128,4,2048]{0,2,1:T(8,128)(2,1)}, u32[]{:S(2)}, u32[]{:S(2)}) async-start(bf16[128,4,2048]{0,2,1:T(8,128)(2,1)} %bitcast.32), calls=%async_computation.3 | async-start | bytes 4194304 | tf_op jit(solution)/shard_map/all_to_all | solution.py:160
  53.8 9.0 %collective-permute-start = (bf16[2,4,128,2,128]{2,4,3,1,0:T(8,128)(2,1)S(1)}, bf16[2,4,128,2,128]{2,4,3,1,0:T(8,128)(2,1)S(1)}, u32[]{:S(2)}, u32[]{:S(2)}) collective-permute-start(bf16[2,4,128,2,128]{2,4,3,1,0:T(8,128)(2,1)S(1)} %pad_maximum_fusion.1), channel_id=1, source_target_pairs={{0,12},{4,16},{8,20},{12,24},{16,28},{20,32},{24,36},{28,40},{32,4... | collective-permute-start | bytes 1572872 | tf_op jit(solution)/shard_map/ppermute | solution.py:22
  62.7 2.2 collective-permute-start.1
  65.0 1.9 collective-permute-start.2
  68.0 8.4 %collective-permute-done = bf16[2,4,128,2,128]{2,4,3,1,0:T(8,128)(2,1)S(1)} collective-permute-done((bf16[2,4,128,2,128]{2,4,3,1,0:T(8,128)(2,1)S(1)}, bf16[2,4,128,2,128]{2,4,3,1,0:T(8,128)(2,1)S(1)}, u32[]{:S(2)}, u32[]{:S(2)}) %collective-permute-start) | collective-permute-done | bytes 524320 | tf_op jit(solution)/shard_map/ppermute | solution.py:22
  76.4 7.8 %collective-permute-done.1 = bf16[2,4,128,2,128]{2,4,3,1,0:T(8,128)(2,1)S(1)} collective-permute-done((bf16[2,4,128,2,128]{2,4,3,1,0:T(8,128)(2,1)S(1)}, bf16[2,4,128,2,128]{2,4,3,1,0:T(8,128)(2,1)S(1)}, u32[]{:S(2)}, u32[]{:S(2)}) %collective-permute-start.1) | collective-permute-done | bytes 524320 | tf_op jit(solution)/shard_map/ppermute | solution.py:22
  84.2 4.7 collective-permute-done.2
  91.3 1.6 broadcast.202
  92.9 1.6 broadcast.202.clone
  94.5 162.5 %while.75 = (s32[]{:T(128)}, bf16[4,128,2,8,128]{4,3,2,1,0:T(8,128)(2,1)}, bf16[4,128,2,8,128]{4,3,2,1,0:T(8,128)(2,1)}, f32[16,128,2,128]{3,1,2,0:T(8,128)}, f3...) while((s32[]{:T(128)}, ...), condition=%wide.region_8.9_spmd.clone, body=%wide.region_2.8_spmd.clone.sunk | while | flops 1985668608 | bytes 74106312 | solution.py:152
  98.3 4.3 fusion.99
  102.7 3.9 broadcast_compare_fusion.5
  107.2 1.5 fusion.100
  110.0 1.8 fusion.101
  111.8 2.6 exponential_reduce_fusion.2
  114.5 3.2 fusion.102
  117.7 1.5 multiply_reduce_fusion.2
  121.2 6.2 %while.76 = (s32[]{:T(128)}, f32[128,2,8,128]{0,3,2,1:T(8,128)S(1)}, f32[16,128,2,128]{3,1,2,0:T(8,128)}, f32[16,128,2,128]{3,1,2,0:T(8,128)}, s32[]{:T(128)}, /...) while((s32[]{:T(128)}, ...), condition=%wide.region_7.7_spmd, body=%wide.region_6.6_spmd.sunk | while | flops 338018304 | bytes 10223873 | solution.py:134
  127.9 1.5 copy.98
  134.3 4.3 fusion.99
  138.7 3.9 broadcast_compare_fusion.5
  143.2 1.5 fusion.100
  146.0 1.8 fusion.101
  147.8 2.6 exponential_reduce_fusion.2
  150.5 3.2 fusion.102
  153.7 1.5 multiply_reduce_fusion.2
  157.2 12.3 %while.76 = (s32[]{:T(128)}, f32[128,2,8,128]{0,3,2,1:T(8,128)S(1)}, f32[16,128,2,128]{3,1,2,0:T(8,128)}, f32[16,128,2,128]{3,1,2,0:T(8,128)}, s32[]{:T(128)}, /...) while((s32[]{:T(128)}, ...), condition=%wide.region_7.7_spmd, body=%wide.region_6.6_spmd.sunk | while | flops 338018304 | bytes 10223873 | solution.py:134
  170.0 1.5 copy.98
  176.4 4.3 fusion.99
  180.8 3.9 broadcast_compare_fusion.5
  185.4 1.5 fusion.100
  188.1 1.8 fusion.101
  190.0 2.6 exponential_reduce_fusion.2
  192.7 3.2 fusion.102
  195.9 1.5 multiply_reduce_fusion.2
  199.3 18.5 %while.76 = (s32[]{:T(128)}, f32[128,2,8,128]{0,3,2,1:T(8,128)S(1)}, f32[16,128,2,128]{3,1,2,0:T(8,128)}, f32[16,128,2,128]{3,1,2,0:T(8,128)}, s32[]{:T(128)}, /...) while((s32[]{:T(128)}, ...), condition=%wide.region_7.7_spmd, body=%wide.region_6.6_spmd.sunk | while | flops 338018304 | bytes 10223873 | solution.py:134
  218.3 1.5 copy.98
  224.8 4.3 fusion.99
  229.1 3.9 broadcast_compare_fusion.5
  233.7 1.5 fusion.100
  236.4 1.8 fusion.101
  238.3 2.6 exponential_reduce_fusion.2
  241.0 3.2 fusion.102
  247.6 6.2 %while.76 = (s32[]{:T(128)}, f32[128,2,8,128]{0,3,2,1:T(8,128)S(1)}, f32[16,128,2,128]{3,1,2,0:T(8,128)}, f32[16,128,2,128]{3,1,2,0:T(8,128)}, s32[]{:T(128)}, /...) while((s32[]{:T(128)}, ...), condition=%wide.region_7.7_spmd, body=%wide.region_6.6_spmd.sunk | while | flops 338018304 | bytes 10223873 | solution.py:134
  254.4 1.5 copy.98
  257.0 3.7 fusion.60
  260.7 24.0 %collective-permute-start.3 = (f32[2,4,128,2,128]{4,2,3,1,0:T(8,128)}, f32[2,4,128,2,128]{4,2,3,1,0:T(8,128)S(1)}, u32[]{:S(2)}, u32[]{:S(2)}) collective-permute-start(f32[2,4,128,2,128]{4,2,3,1,0:T(8,128)} %get-tuple-element.866), channel_id=1, source_target_pairs={{12,0},{16,4},{20,8},{24,12},{28,16},{32,20},{36,24},{40,28},{44,3... | collective-permute-start | bytes 3145736 | tf_op jit(solution)/shard_map/ppermute | solution.py:22
  284.7 98.9 %collective-permute-start.4 = (f32[2,4,128,2,128]{4,2,3,1,0:T(8,128)}, f32[2,4,128,2,128]{4,2,3,1,0:T(8,128)}, u32[]{:S(2)}, u32[]{:S(2)}) collective-permute-start(f32[2,4,128,2,128]{4,2,3,1,0:T(8,128)} %get-tuple-element.868), channel_id=1, source_target_pairs={{8,0},{12,4},{16,8},{20,12},{24,16},{28,20},{32,24},{36,28},{40,32... | collective-permute-start | bytes 3145736 | tf_op jit(solution)/shard_map/ppermute | solution.py:22
  383.6 101.6 %collective-permute-start.5 = (f32[2,4,128,2,128]{4,2,3,1,0:T(8,128)}, f32[2,4,128,2,128]{4,2,3,1,0:T(8,128)}, u32[]{:S(2)}, u32[]{:S(2)}) collective-permute-start(f32[2,4,128,2,128]{4,2,3,1,0:T(8,128)} %get-tuple-element.867), channel_id=1, source_target_pairs={{4,0},{8,4},{12,8},{16,12},{20,16},{24,20},{28,24},{32,28},{36,32}... | collective-permute-start | bytes 3145736 | tf_op jit(solution)/shard_map/ppermute | solution.py:22
  485.2 2.3 reshape.209
  487.5 4.3 reshape.210
  491.8 34.5 %collective-permute-done.4 = f32[2,4,128,2,128]{4,2,3,1,0:T(8,128)} collective-permute-done((f32[2,4,128,2,128]{4,2,3,1,0:T(8,128)}, f32[2,4,128,2,128]{4,2,3,1,0:T(8,128)}, u32[]{:S(2)}, u32[]{:S(2)}) %collective-permute-start.4) | collective-permute-done | bytes 1048608 | tf_op jit(solution)/shard_map/ppermute | solution.py:22
  526.3 2.6 collective-permute-done.5
  528.8 2.0 fusion.59
  (173 shorter events, 63.0 us)
Async XLA Ops:
  0.6 15.2 %copy-start.3 = (bf16[128,8192]{1,0:T(8,128)(2,1)S(1)}, bf16[128,8192]{1,0:T(8,128)(2,1)}, u32[]{:S(2)}) copy-start(bf16[128,8192]{1,0:T(8,128)(2,1)} %param.11) | copy-start | bytes 6291460
  2.6 8.8 %all-to-all-start = ((bf16[128,4,256]{0,2,1:T(8,128)(2,1)}), bf16[128,4,256]{0,2,1:T(8,128)(2,1)S(1)}, u32[]{:S(2)}, u32[]{:S(2)}) async-start(bf16[128,4,256]{0,2,1:T(8,128)(2,1)} %bitcast.20), calls=%async_computation | async-start | bytes 524288 | tf_op jit(solution)/shard_map/all_to_all | solution.py:158
  11.3 8.9 %all-to-all-start.1 = ((bf16[128,4,256]{0,2,1:T(8,128)(2,1)}), bf16[128,4,256]{0,2,1:T(8,128)(2,1)S(1)}, u32[]{:S(2)}, u32[]{:S(2)}) async-start(bf16[128,4,256]{0,2,1:T(8,128)(2,1)} %bitcast.23), calls=%async_computation.1 | async-start | bytes 524288 | tf_op jit(solution)/shard_map/all_to_all | solution.py:159
  20.2 5.7 %copy-start.4 = (bf16[128,8192]{1,0:T(8,128)(2,1)S(1)}, bf16[128,8192]{1,0:T(8,128)(2,1)}, u32[]{:S(2)}) copy-start(bf16[128,8192]{1,0:T(8,128)(2,1)} %param.14) | copy-start | bytes 6291460
  20.2 27.8 %all-to-all-start.2 = ((bf16[128,4,2048]{0,2,1:T(8,128)(2,1)}), bf16[128,4,2048]{0,2,1:T(8,128)(2,1)}, u32[]{:S(2)}, u32[]{:S(2)}) async-start(bf16[128,4,2048]{0,2,1:T(8,128)(2,1)} %bitcast.29), calls=%async_computation.2 | async-start | bytes 4194304 | tf_op jit(solution)/shard_map/all_to_all | solution.py:157
  48.0 18.9 %copy-start.6 = (s32[16]{0:T(128)S(1)}, s32[16]{0:T(128)}, u32[]{:S(2)}) copy-start(s32[16]{0:T(128)} %param.15) | copy-start | bytes 196
  48.0 43.3 %all-to-all-start.3 = ((bf16[128,4,2048]{0,2,1:T(8,128)(2,1)}), bf16[128,4,2048]{0,2,1:T(8,128)(2,1)}, u32[]{:S(2)}, u32[]{:S(2)}) async-start(bf16[128,4,2048]{0,2,1:T(8,128)(2,1)} %bitcast.32), calls=%async_computation.3 | async-start | bytes 4194304 | tf_op jit(solution)/shard_map/all_to_all | solution.py:160
  53.8 22.6 %collective-permute-start = (bf16[2,4,128,2,128]{2,4,3,1,0:T(8,128)(2,1)S(1)}, bf16[2,4,128,2,128]{2,4,3,1,0:T(8,128)(2,1)S(1)}, u32[]{:S(2)}, u32[]{:S(2)}) collective-permute-start(bf16[2,4,128,2,128]{2,4,3,1,0:T(8,128)(2,1)S(1)} %pad_maximum_fusion.1), channel_id=1, source_target_pairs={{0,12},{4,16},{8,20},{12,24},{16,28},{20,32},{24,36},{28,40},{32,4... | collective-permute-start | bytes 1572872 | tf_op jit(solution)/shard_map/ppermute | solution.py:22
  62.7 21.5 %collective-permute-start.1 = (bf16[2,4,128,2,128]{2,4,3,1,0:T(8,128)(2,1)S(1)}, bf16[2,4,128,2,128]{2,4,3,1,0:T(8,128)(2,1)S(1)}, u32[]{:S(2)}, u32[]{:S(2)}) collective-permute-start(bf16[2,4,128,2,128]{2,4,3,1,0:T(8,128)(2,1)S(1)} %pad_maximum_fusion.1), channel_id=1, source_target_pairs={{0,8},{4,12},{8,16},{12,20},{16,24},{20,28},{24,32},{28,36},{32,40... | collective-permute-start | bytes 1572872 | tf_op jit(solution)/shard_map/ppermute | solution.py:22
  65.0 23.9 %collective-permute-start.2 = (bf16[2,4,128,2,128]{2,4,3,1,0:T(8,128)(2,1)S(1)}, bf16[2,4,128,2,128]{2,4,3,1,0:T(8,128)(2,1)S(1)}, u32[]{:S(2)}, u32[]{:S(2)}) collective-permute-start(bf16[2,4,128,2,128]{2,4,3,1,0:T(8,128)(2,1)S(1)} %pad_maximum_fusion.1), channel_id=1, source_target_pairs={{0,4},{4,8},{8,12},{12,16},{16,20},{20,24},{24,28},{28,32},{32,36}... | collective-permute-start | bytes 1572872 | tf_op jit(solution)/shard_map/ppermute | solution.py:22
  111.8 2.6 copy-start.2
  117.7 1.5 copy-start
  147.8 2.6 copy-start.2
  153.7 1.5 copy-start
  190.0 2.6 copy-start.2
  195.9 1.5 copy-start
  238.3 2.6 copy-start.2
  244.2 1.5 copy-start
  257.0 228.2 %copy-start.5 = (bf16[4,128,2,8,128]{4,3,2,1,0:T(8,128)(2,1)S(1)}, bf16[4,128,2,8,128]{4,3,2,1,0:T(8,128)(2,1)}, u32[]{:S(2)}) copy-start(bf16[4,128,2,8,128]{4,3,2,1,0:T(8,128)(2,1)} %get-tuple-element.604) | copy-start | bytes 6291460
  260.7 231.1 %collective-permute-start.3 = (f32[2,4,128,2,128]{4,2,3,1,0:T(8,128)}, f32[2,4,128,2,128]{4,2,3,1,0:T(8,128)S(1)}, u32[]{:S(2)}, u32[]{:S(2)}) collective-permute-start(f32[2,4,128,2,128]{4,2,3,1,0:T(8,128)} %get-tuple-element.866), channel_id=1, source_target_pairs={{12,0},{16,4},{20,8},{24,12},{28,16},{32,20},{36,24},{40,28},{44,3... | collective-permute-start | bytes 3145736 | tf_op jit(solution)/shard_map/ppermute | solution.py:22
  284.7 241.6 %collective-permute-start.4 = (f32[2,4,128,2,128]{4,2,3,1,0:T(8,128)}, f32[2,4,128,2,128]{4,2,3,1,0:T(8,128)}, u32[]{:S(2)}, u32[]{:S(2)}) collective-permute-start(f32[2,4,128,2,128]{4,2,3,1,0:T(8,128)} %get-tuple-element.868), channel_id=1, source_target_pairs={{8,0},{12,4},{16,8},{20,12},{24,16},{28,20},{32,24},{36,28},{40,32... | collective-permute-start | bytes 3145736 | tf_op jit(solution)/shard_map/ppermute | solution.py:22
  383.6 145.3 %collective-permute-start.5 = (f32[2,4,128,2,128]{4,2,3,1,0:T(8,128)}, f32[2,4,128,2,128]{4,2,3,1,0:T(8,128)}, u32[]{:S(2)}, u32[]{:S(2)}) collective-permute-start(f32[2,4,128,2,128]{4,2,3,1,0:T(8,128)} %get-tuple-element.867), channel_id=1, source_target_pairs={{4,0},{8,4},{12,8},{16,12},{20,16},{24,20},{28,24},{32,28},{36,32}... | collective-permute-start | bytes 3145736 | tf_op jit(solution)/shard_map/ppermute | solution.py:22
  487.5 41.4 %copy-start.1 = (f32[16,128,2,128]{3,1,2,0:T(8,128)S(1)}, f32[16,128,2,128]{3,1,2,0:T(8,128)}, u32[]{:S(2)}) copy-start(f32[16,128,2,128]{3,1,2,0:T(8,128)} %get-tuple-element.606) | copy-start | bytes 6291460
where the time goes:
time: 538 us; the launch traced here: 532 us
  starting transfers between devices  258 us (48%)
  waiting for transfers between devices  82.1 us (15%)
  other arithmetic  64.7 us (12%)
  local copies, waits for them, and re-layouts  54.8 us (10%)
  matrix products  47 us (9%)
  loops' own time  25 us (5%)
    ppermute x6, starting transfers between devices, from_behind(): lax.ppermute(value, axis, [(source, source + steps) for source in range(f...  238 us
    ppermute x6, waiting for transfers between devices, from_behind(): lax.ppermute(value, axis, [(source, source + steps) for source in range(f...  57.9 us
    all_to_all x1, waiting for transfers between devices, shards(): lax.all_to_all(queries, 'head', split_axis=1, concat_axis=0, tiled=True)  19.6 us
    gather x8, other arithmetic, attend(): jnp.repeat(jnp.arange(span_tiles, dtype=jnp.int32), block_len, total_repe...  17.5 us
    another operation x1, loops' own time, attend(): return lax.fori_loop(0, query_blocks.shape[0], one_block, initial)  15.8 us
    ge x4, other arithmetic, one_block(): sources[None, :] >= doc_start  15.5 us
    dot_general x4, matrix products, one_block(): jnp.einsum('hgqk,khd->qhgd', span_rounded, value_span, preferred_element_...  12.7 us
  transfers between devices with their start and end apart: 10, of which 8 were waited for; matrix products, arithmetic and copies ran while one was open for 3% of the time, Pallas kernels for 0%

commit v1 on v0

v1 whole, which is shorter than its diff:
```python
import math

import jax
import jax.numpy as jnp
from jax import lax
from jax.experimental import pallas as pl
from jax.experimental.pallas import tpu as pltpu
from jax.sharding import PartitionSpec as P

HQ = 64
HK = 8
DH = 128
BLOCK = 128
MAXDOC = 12
DOCS = 16

CTX = 32
HEADS = 4
GROUP = HQ // HK
KV = HK // HEADS
SHARD = 4
SLOTS = 16
SPAN = MAXDOC * BLOCK
QCOLS = GROUP * DH

INV = 1.0 / math.sqrt(DH)
EXP2_SCALE = INV * math.log2(math.e)
MASKED = -1e30

MESH = pl.DeviceIdType.MESH
NN = (((1,), (0,)), ((), ()))
NT = (((1,), (1,)), ((), ()))
TN = (((0,), (0,)), ((), ()))


def dot(a, b, dims):
    return lax.dot_general(a, b, dims, preferred_element_type=jnp.float32)


def rows(first_block, blocks):
    start = first_block * BLOCK
    if not isinstance(first_block, int):
        start = pl.multiple_of(start, BLOCK)
    return pl.ds(start, blocks * BLOCK)


def columns(first, width):
    return pl.ds(pl.multiple_of(first, BLOCK), width)


def kernel(
    docs, q_in, k_in, v_in, g_in, o_out, dq_out, dk_out, dv_out,
    q_buf, g_buf, kv_buf, dk_acc, dv_acc, part, landed, p_buf, ds_buf, gs_buf,
    kv_send, kv_recv, fwd_send, fwd_recv, q_send, q_recv, part_send, part_recv,
):
    c = lax.axis_index("ctx")
    h = lax.axis_index("head")
    parity = lax.rem(c, 2)

    def ctx_at(delta):
        return lax.rem(c + (delta + CTX), CTX)

    def head_at(step):
        return lax.rem(h + step, HEADS)

    barrier = pltpu.get_barrier_semaphore()
    for step in range(1, HEADS):
        pl.semaphore_signal(barrier, inc=1, device_id=(c, head_at(step)), device_id_type=MESH)
    for delta in (-3, -2, -1, 1, 2, 3):
        pl.semaphore_signal(barrier, inc=1, device_id=(ctx_at(delta), h), device_id_type=MESH)
    pl.semaphore_wait(barrier, 9)

    def kv_copy(which, step):
        source = (k_in, v_in)[which]
        peer = head_at(step)
        src = source.at[:, columns(peer * (KV * DH), KV * DH)]
        dst = kv_buf.at[which, rows(12 + h, 1), :]
        if step == 0:
            return pltpu.make_async_copy(src, dst, kv_recv.at[which, 0])
        return pltpu.make_async_remote_copy(
            src, dst, kv_send.at[which, step], kv_recv.at[which, step],
            device_id=(c, peer), device_id_type=MESH,
        )

    def qg_copy(which, group, step):
        source, target = ((q_in, q_buf), (g_in, g_buf))[which]
        peer = head_at(step)
        src = source.at[:, columns(peer * (KV * QCOLS) + group * QCOLS, QCOLS)]
        dst = target.at[h, :, pl.ds(group * QCOLS, QCOLS)]
        if step == 0:
            return pltpu.make_async_copy(src, dst, q_recv.at[which, group, 0])
        return pltpu.make_async_remote_copy(
            src, dst, q_send.at[which, group, step], q_recv.at[which, group, step],
            device_id=(c, peer), device_id_type=MESH,
        )

    def shard_copy(index, src_block, dst_block, blocks, delta):
        return pltpu.make_async_remote_copy(
            kv_buf.at[:, rows(src_block, blocks), :],
            kv_buf.at[:, rows(dst_block, blocks), :],
            fwd_send.at[index], fwd_recv.at[index],
            device_id=(ctx_at(delta), h), device_id_type=MESH,
        )

    own_next = lambda: shard_copy(1, 12, 8, 4, 1)
    own_two = lambda: shard_copy(2, 12, 4, 4, 2)
    own_three = lambda: shard_copy(3, 13, 1, 3, 3)
    pass_next = lambda: shard_copy(3, 5, 1, 3, 1)
    pass_back = lambda: shard_copy(1, 4, 8, 4, -1)

    for step in (1, 3, 2, 0):
        for which in range(2):
            kv_copy(which, step).start()
    for group in range(KV):
        for step in (0, 1, 3, 2):
            for which in range(2):
                qg_copy(which, group, step).start()

    dk_acc[...] = jnp.zeros_like(dk_acc)
    dv_acc[...] = jnp.zeros_like(dv_acc)

    firsts = []
    for b in range(SHARD):
        block = c * SHARD + b
        begin = jnp.int32(0)
        first = jnp.int32(0)
        for d in range(DOCS):
            end = begin + docs[d]
            first = jnp.where((block >= begin) & (block < end), begin, first)
            begin = end
        firsts.append(first - (block - (MAXDOC - 1)))

    for step in range(HEADS):
        for which in range(2):
            if step == 0:
                kv_copy(which, step).wait()
            else:
                kv_copy(which, step).wait_recv()

    own_two().start()

    @pl.when(parity == 0)
    def _():
        own_next().start()

    @pl.when(parity == 1)
    def _():
        own_three().start()

    own_two().wait_recv()

    @pl.when(parity == 0)
    def _():
        pass_next().start()

    @pl.when(parity == 1)
    def _():
        pass_back().start()

    own_next().wait_recv()
    own_three().wait_recv()

    def part_copy(group, delta):
        blocks = 3 if delta == 3 else 4
        source = 1 if delta == 3 else 12 - 4 * delta
        target = 1 if delta == 3 else 0
        return pltpu.make_async_remote_copy(
            part.at[:, group, rows(source, blocks), :],
            landed.at[delta - 1, :, group, rows(target, blocks), :],
            part_send.at[group, delta - 1], part_recv.at[group, delta - 1],
            device_id=(ctx_at(-delta), h), device_id_type=MESH,
        )

    tri = lax.broadcasted_iota(jnp.int32, (QCOLS, BLOCK), 1) <= (
        lax.broadcasted_iota(jnp.int32, (QCOLS, BLOCK), 0) & (BLOCK - 1)
    )

    def unit(index, _):
        group = index // HEADS
        step = lax.rem(index, HEADS)
        b = lax.rem(h + HEADS - step, HEADS)
        for which, buf in ((0, q_buf), (1, g_buf)):
            here = buf.at[b, :, columns(group * QCOLS, QCOLS)]
            pltpu.make_async_copy(here, here, q_recv.at[which, group, step]).wait()
        low = firsts[0]
        for other in range(1, SHARD):
            low = jnp.where(b == other, firsts[other], low)
        window = pl.ds(pl.multiple_of((b + 1) * BLOCK, BLOCK), SPAN)
        features = columns(group * DH, DH)
        k = kv_buf[0, window, features]
        v = kv_buf[1, window, features]
        heads = [columns(group * QCOLS + i * DH, DH) for i in range(GROUP)]
        q = jnp.concatenate([q_buf[b, :, at] for at in heads], 0)
        grad = jnp.concatenate([g_buf[b, :, at] for at in heads], 0)
        s = dot(q, k, NT)
        tiles = []
        for j in range(MAXDOC):
            tile = s[:, j * BLOCK : (j + 1) * BLOCK]
            keep = tri if j == MAXDOC - 1 else low <= j
            tiles.append(jnp.where(keep, tile, MASKED))
        top = tiles[0]
        for tile in tiles[1:]:
            top = jnp.maximum(top, tile)
        top = jnp.max(top, axis=1, keepdims=True) * EXP2_SCALE
        total = None
        weights = []
        for tile in tiles:
            p = jnp.exp2(tile * EXP2_SCALE - top)
            total = p if total is None else total + p
            weights.append(p.astype(jnp.bfloat16))
        scale = 1.0 / jnp.sum(total, axis=1, keepdims=True)
        p_all = jnp.concatenate(weights, 1)
        p_buf[...] = p_all
        out = (dot(p_all, v, NN) * scale).astype(jnp.bfloat16)
        grad_f = grad.astype(jnp.float32)
        delta = jnp.sum(grad_f * out.astype(jnp.float32), axis=1, keepdims=True) * scale
        grad_s = (grad_f * scale).astype(jnp.bfloat16)
        gs_buf[...] = grad_s
        dp = dot(grad_s, v, NT)
        terms = []
        for j in range(MAXDOC):
            inner = dp[:, j * BLOCK : (j + 1) * BLOCK] - delta
            terms.append((weights[j].astype(jnp.float32) * inner).astype(jnp.bfloat16))
        ds = jnp.concatenate(terms, 1)
        ds_buf[...] = ds
        dq = (dot(ds, k, NN) * INV).astype(jnp.bfloat16)
        for i, at in enumerate(heads):
            o_out[b, :, at] = out[i * BLOCK : (i + 1) * BLOCK]
            dq_out[b, :, at] = dq[i * BLOCK : (i + 1) * BLOCK]
        dv_acc[group, window, :] += dot(p_buf[...], gs_buf[...], TN)
        dk_acc[group, window, :] += dot(ds_buf[...], q, TN)

        @pl.when(step == HEADS - 1)
        def _():
            part[0, group] = (dk_acc[group, : 12 * BLOCK, :] * INV).astype(jnp.bfloat16)
            part[1, group] = dv_acc[group, : 12 * BLOCK, :].astype(jnp.bfloat16)
            for delta in (1, 2, 3):
                part_copy(group, delta).start()

        return 0

    lax.fori_loop(0, KV * HEADS, unit, 0)

    for group in range(KV):
        for delta in (1, 2, 3):
            part_copy(group, delta).wait_recv()
        lanes = slice(group * DH, (group + 1) * DH)
        for which, acc, out in ((0, dk_acc, dk_out), (1, dv_acc, dv_out)):
            for block in range(SHARD):
                at = slice(block * BLOCK, (block + 1) * BLOCK)
                total = acc[group, (12 + block) * BLOCK : (13 + block) * BLOCK, :]
                if which == 0:
                    total = total * INV
                for delta in (1, 2, 3):
                    if delta < 3 or block > 0:
                        total = total + landed[delta - 1, which, group, at, :].astype(jnp.float32)
                out[at, lanes] = total.astype(jnp.bfloat16)

    for step in range(1, HEADS):
        for which in range(2):
            kv_copy(which, step).wait_send()
            for group in range(KV):
                qg_copy(which, group, step).wait_send()
    own_two().wait_send()

    @pl.when(parity == 0)
    def _():
        own_next().wait_send()
        pass_next().wait_send()

    @pl.when(parity == 1)
    def _():
        own_three().wait_send()
        pass_back().wait_send()

    for group in range(KV):
        for delta in (1, 2, 3):
            part_copy(group, delta).wait_send()


def shards(queries, key_states, value_states, out_grads, doc_blocks):
    bf16, f32 = jnp.bfloat16, jnp.float32
    anywhere = pl.BlockSpec(memory_space=pl.ANY)
    vmem = pl.BlockSpec(memory_space=pltpu.VMEM)
    dma = pltpu.SemaphoreType.DMA
    tokens = SHARD * BLOCK
    out, dq, dk, dv = pl.pallas_call(
        kernel,
        out_shape=[
            jax.ShapeDtypeStruct((SHARD, BLOCK, KV * QCOLS), bf16),
            jax.ShapeDtypeStruct((SHARD, BLOCK, KV * QCOLS), bf16),
            jax.ShapeDtypeStruct((tokens, KV * DH), bf16),
            jax.ShapeDtypeStruct((tokens, KV * DH), bf16),
        ],
        in_specs=[pl.BlockSpec(memory_space=pltpu.SMEM)] + [anywhere] * 4,
        out_specs=[vmem] * 4,
        scratch_shapes=[
            pltpu.VMEM((SHARD, BLOCK, KV * QCOLS), bf16),
            pltpu.VMEM((SHARD, BLOCK, KV * QCOLS), bf16),
            pltpu.VMEM((2, SLOTS * BLOCK, KV * DH), bf16),
            pltpu.VMEM((KV, SLOTS * BLOCK, DH), f32),
            pltpu.VMEM((KV, SLOTS * BLOCK, DH), f32),
            pltpu.VMEM((2, KV, 12 * BLOCK, DH), bf16),
            pltpu.VMEM((3, 2, KV, tokens, DH), bf16),
            pltpu.VMEM((QCOLS, SPAN), bf16),
            pltpu.VMEM((QCOLS, SPAN), bf16),
            pltpu.VMEM((QCOLS, DH), bf16),
            dma((2, HEADS)), dma((2, HEADS)),
            dma((4,)), dma((4,)),
            dma((2, KV, HEADS)), dma((2, KV, HEADS)),
            dma((KV, 3)), dma((KV, 3)),
        ],
        compiler_params=pltpu.CompilerParams(
            collective_id=0, has_side_effects=True, vmem_limit_bytes=60 * 2**20
        ),
        name="attention",
    )(doc_blocks, queries, key_states, value_states, out_grads)
    width = KV * QCOLS
    return out.reshape(tokens, width), dq.reshape(tokens, width), dk, dv


def solution(mesh):
    entry = P(("ctx", "head"), None)
    return jax.shard_map(
        shards,
        mesh=mesh,
        in_specs=(entry, entry, entry, entry, P()),
        out_specs=(P("ctx", "head"),) * 4,
        check_vma=False,
    )
```

time: 538 us -> 111 us (0.21)
  the two profiles are of different devices: /device:TPU:41 before, /device:TPU:6 now
where the time goes in v1:
time: 111 us
  Pallas kernels  104 us (94%)
  local copies, waits for them, and re-layouts  6.04 us (5%)
    pallas_call x1, Pallas kernels, shards(): pl.pallas_call(kernel, out_shape=[jax.ShapeDtypeStruct((SHARD, BLOCK, KV...  104 us
    unnamed x10, local copies, waits for them, and re-layouts  6.04 us

profile of v1, /device:TPU:6, one launch (start us, length us, event | category | flops | bytes accessed | tf_op | source)
XLA Modules:
  0.0 110.6 jit_solution(8354214512906079197)
XLA Ops:
  0.6 103.9 %attention.1 = (bf16[4,128,2048]{2,1,0:T(8,128)(2,1)}, bf16[4,128,2048]{2,1,0:T(8,128)(2,1)}, bf16[512,256]{1,0:T(8,128)(2,1)}, bf16[512,256]{1,0:T(8,128)(2,1)}) custom-call(s32[16]{0:T(128)} %docs.1, bf16[128,8192]{1,0:T(8,128)(2,1)} %q_in.1, bf16[128,1024]{1,0:T(8,128)(2,1)} %k_in.1, bf16[128,1024]{1,0:T(8,128)(2,1)} %v_in.1, bf16[128,8192]{1,0:T(8,128)(2,1)} %g_in.1), custom_call_target="tpu_custom_call" | custom-call | tf_op jit(solution)/shard_map/attention/pallas_call | solution.py:287
  104.6 0.0 copy-start
  104.6 3.3 %copy.13 = bf16[512,2048]{1,0:T(8,128)(2,1)} copy(bf16[512,2048]{1,0:T(8,128)(2,1)} %bitcast.3) | data formatting | bytes 4194304
  107.9 0.0 copy-done
  107.9 0.0 copy-start.2
  107.9 0.0 copy-start.1
  107.9 1.3 %copy.14 = bf16[512,2048]{1,0:T(8,128)(2,1)} copy(bf16[512,2048]{1,0:T(8,128)(2,1)S(1)} %bitcast.2) | data formatting | bytes 4194304
  109.2 0.0 copy-done.2
  109.2 0.7 copy.15
  109.9 0.0 copy-done.1
  109.9 0.7 copy.16
Async XLA Ops:
  104.6 3.3 %copy-start = (bf16[4,128,2048]{2,1,0:T(8,128)(2,1)S(1)}, bf16[4,128,2048]{2,1,0:T(8,128)(2,1)}, u32[]{:S(2)}) copy-start(bf16[4,128,2048]{2,1,0:T(8,128)(2,1)} %get-tuple-element.9) | copy-start | bytes 6291460
  107.9 1.3 %copy-start.2 = (bf16[512,256]{1,0:T(8,128)(2,1)S(1)}, bf16[512,256]{1,0:T(8,128)(2,1)}, u32[]{:S(2)}) copy-start(bf16[512,256]{1,0:T(8,128)(2,1)} %get-tuple-element.18) | copy-start | bytes 786436
  107.9 2.0 %copy-start.1 = (bf16[512,256]{1,0:T(8,128)(2,1)S(1)}, bf16[512,256]{1,0:T(8,128)(2,1)}, u32[]{:S(2)}) copy-start(bf16[512,256]{1,0:T(8,128)(2,1)} %get-tuple-element.19) | copy-start | bytes 786436

commit v2 on v1

--- a/solution.py
+++ b/solution.py
@@ -22,6 +22,7 @@
 SLOTS = 16
 SPAN = MAXDOC * BLOCK
 QCOLS = GROUP * DH
+PIECES = ((1, 2, 3), (3, 1, 3), (4, 4, 2), (8, 4, 1))
 
 INV = 1.0 / math.sqrt(DH)
 EXP2_SCALE = INV * math.log2(math.e)
@@ -94,19 +95,19 @@
             device_id=(c, peer), device_id_type=MESH,
         )
 
-    def shard_copy(index, src_block, dst_block, blocks, delta):
+    def block_copy(kind, step, src_slot, dst_slot, delta):
+        b = lax.rem(h + HEADS - step, HEADS)
         return pltpu.make_async_remote_copy(
-            kv_buf.at[:, rows(src_block, blocks), :],
-            kv_buf.at[:, rows(dst_block, blocks), :],
-            fwd_send.at[index], fwd_recv.at[index],
+            kv_buf.at[:, rows(src_slot + b, 1), :],
+            kv_buf.at[:, rows(dst_slot + b, 1), :],
+            fwd_send.at[kind, step], fwd_recv.at[kind, step],
             device_id=(ctx_at(delta), h), device_id_type=MESH,
         )
 
-    own_next = lambda: shard_copy(1, 12, 8, 4, 1)
-    own_two = lambda: shard_copy(2, 12, 4, 4, 2)
-    own_three = lambda: shard_copy(3, 13, 1, 3, 3)
-    pass_next = lambda: shard_copy(3, 5, 1, 3, 1)
-    pass_back = lambda: shard_copy(1, 4, 8, 4, -1)
+    to_sibling = lambda step: block_copy(0, step, 12, 8, 1)
+    back_sibling = lambda step: block_copy(0, step, 4, 8, -1)
+    to_second = lambda step: block_copy(1, step, 12, 4, 2)
+    pass_third = lambda step: block_copy(2, step, 4, 0, 1)
 
     for step in (1, 3, 2, 0):
         for which in range(2):
@@ -130,54 +131,75 @@
             begin = end
         firsts.append(first - (block - (MAXDOC - 1)))
 
-    for step in range(HEADS):
+    def send_own(step):
         for which in range(2):
             if step == 0:
                 kv_copy(which, step).wait()
             else:
                 kv_copy(which, step).wait_recv()
-
-    own_two().start()
-
-    @pl.when(parity == 0)
-    def _():
-        own_next().start()
-
-    @pl.when(parity == 1)
-    def _():
-        own_three().start()
-
-    own_two().wait_recv()
-
-    @pl.when(parity == 0)
-    def _():
-        pass_next().start()
-
-    @pl.when(parity == 1)
-    def _():
-        pass_back().start()
-
-    own_next().wait_recv()
-    own_three().wait_recv()
-
-    def part_copy(group, delta):
-        blocks = 3 if delta == 3 else 4
-        source = 1 if delta == 3 else 12 - 4 * delta
-        target = 1 if delta == 3 else 0
+        to_second(step).start()
+
+        @pl.when(parity == 0)
+        def _():
+            to_sibling(step).start()
+
+    def send_on(step):
+        to_second(step).wait_recv()
+
+        @pl.when(h != step)
+        def _():
+            pass_third(step).start()
+
+        @pl.when(parity == 1)
+        def _():
+            back_sibling(step).start()
+
+    send_own(0)
+    send_own(1)
+    send_on(0)
+    send_own(3)
+    send_on(1)
+    send_own(2)
+    send_on(3)
+    send_on(2)
+    for step in range(HEADS):
+        to_sibling(step).wait_recv()
+
+        @pl.when(h != step)
+        def _():
+            pass_third(step).wait_recv()
+
+    def part_copy(which, group, piece):
+        first, blocks, delta = PIECES[piece]
         return pltpu.make_async_remote_copy(
-            part.at[:, group, rows(source, blocks), :],
-            landed.at[delta - 1, :, group, rows(target, blocks), :],
-            part_send.at[group, delta - 1], part_recv.at[group, delta - 1],
+            part.at[which, group, :, pl.ds(first * BLOCK, blocks * BLOCK)],
+            landed.at[which, group, delta - 1, :, pl.ds(first % SHARD * BLOCK, blocks * BLOCK)],
+            part_send.at[which, group, piece], part_recv.at[which, group, piece],
             device_id=(ctx_at(-delta), h), device_id_type=MESH,
         )
+
+    def send_parts(which, group, pieces):
+        for piece in pieces:
+            first, blocks, _ = PIECES[piece]
+            lanes = slice(first * BLOCK, (first + blocks) * BLOCK)
+            total = (dk_acc, dv_acc)[which][group, :, lanes]
+            if which == 0:
+                total = total * INV
+            part[which, group, :, lanes] = total.astype(jnp.bfloat16)
+            part_copy(which, group, piece).start()
 
     tri = lax.broadcasted_iota(jnp.int32, (QCOLS, BLOCK), 1) <= (
         lax.broadcasted_iota(jnp.int32, (QCOLS, BLOCK), 0) & (BLOCK - 1)
     )
 
-    def unit(index, _):
-        group = index // HEADS
-        step = lax.rem(index, HEADS)
+    def unit(index, _, last=False):
+        early = 1 - (index + 6) // 8
+        group = early * index + (1 - early) * ((index + 1) // 3 - 1)
+        turn = lax.rem(index + 1, 3)
+        usual = 1 + lax.rem(2 * turn, 3)
+        inner = (h * (3 - h)) // 2
+        ending = (1 - inner) * (3 - turn) + inner * ((h - 1) * (1 + turn) + (2 - h) * usual)
+        step = (1 - early) * ((1 - group) * usual + group * ending)
         b = lax.rem(h + HEADS - step, HEADS)
         for which, buf in ((0, q_buf), (1, g_buf)):
             here = buf.at[b, :, columns(group * QCOLS, QCOLS)]
@@ -211,11 +233,16 @@
         scale = 1.0 / jnp.sum(total, axis=1, keepdims=True)
         p_all = jnp.concatenate(weights, 1)
         p_buf[...] = p_all
-        out = (dot(p_all, v, NN) * scale).astype(jnp.bfloat16)
+        out = (dot(v.T, p_all.T, NN).T * scale).astype(jnp.bfloat16)
         grad_f = grad.astype(jnp.float32)
         delta = jnp.sum(grad_f * out.astype(jnp.float32), axis=1, keepdims=True) * scale
         grad_s = (grad_f * scale).astype(jnp.bfloat16)
         gs_buf[...] = grad_s
+        for i, at in enumerate(heads):
+            o_out[b, :, at] = out[i * BLOCK : (i + 1) * BLOCK]
+        if last:
+            dv_acc[group, :, window] += dot(gs_buf[...], p_buf[...], TN)
+            send_parts(1, 1, (2, 1, 3))
         dp = dot(grad_s, v, NT)
         terms = []
         for j in range(MAXDOC):
@@ -223,59 +250,63 @@
             terms.append((weights[j].astype(jnp.float32) * inner).astype(jnp.bfloat16))
         ds = jnp.concatenate(terms, 1)
         ds_buf[...] = ds
+        if last:
+            dk_acc[group, :, window] += dot(q, ds_buf[...], TN)
+            send_parts(0, 1, (2, 1, 3))
         dq = (dot(ds, k, NN) * INV).astype(jnp.bfloat16)
         for i, at in enumerate(heads):
-            o_out[b, :, at] = out[i * BLOCK : (i + 1) * BLOCK]
             dq_out[b, :, at] = dq[i * BLOCK : (i + 1) * BLOCK]
-        dv_acc[group, window, :] += dot(p_buf[...], gs_buf[...], TN)
-        dk_acc[group, window, :] += dot(ds_buf[...], q, TN)
-
-        @pl.when(step == HEADS - 1)
-        def _():
-            part[0, group] = (dk_acc[group, : 12 * BLOCK, :] * INV).astype(jnp.bfloat16)
-            part[1, group] = dv_acc[group, : 12 * BLOCK, :].astype(jnp.bfloat16)
-            for delta in (1, 2, 3):
-                part_copy(group, delta).start()
+        if last:
+            return
+        dv_acc[group, :, window] += dot(gs_buf[...], p_buf[...], TN)
+        dk_acc[group, :, window] += dot(q, ds_buf[...], TN)
+
+        @pl.when(index == HEADS)
+        def _():
+            for which in (1, 0):
+                send_parts(which, 0, (0, 1, 2, 3))
 
         return 0
 
-    lax.fori_loop(0, KV * HEADS, unit, 0)
+    lax.fori_loop(0, KV * HEADS - 1, unit, 0)
+    send_parts(1, 1, (0,))
+    send_parts(0, 1, (0,))
+    unit(KV * HEADS - 1, 0, last=True)
 
     for group in range(KV):
-        for delta in (1, 2, 3):
-            part_copy(group, delta).wait_recv()
+        for which in range(2):
+            for piece in range(len(PIECES)):
+                part_copy(which, group, piece).wait_recv()
         lanes = slice(group * DH, (group + 1) * DH)
         for which, acc, out in ((0, dk_acc, dk_out), (1, dv_acc, dv_out)):
             for block in range(SHARD):
                 at = slice(block * BLOCK, (block + 1) * BLOCK)
-                total = acc[group, (12 + block) * BLOCK : (13 + block) * BLOCK, :]
+                total = acc[group, :, (12 + block) * BLOCK : (13 + block) * BLOCK]
                 if which == 0:
                     total = total * INV
                 for delta in (1, 2, 3):
                     if delta < 3 or block > 0:
-                        total = total + landed[delta - 1, which, group, at, :].astype(jnp.float32)
-                out[at, lanes] = total.astype(jnp.bfloat16)
+                        total = total + landed[which, group, delta - 1, :, at].astype(jnp.float32)
+                out[at, lanes] = total.T.astype(jnp.bfloat16)
 
     for step in range(1, HEADS):
         for which in range(2):
             kv_copy(which, step).wait_send()
             for group in range(KV):
                 qg_copy(which, group, step).wait_send()
-    own_two().wait_send()
-
-    @pl.when(parity == 0)
-    def _():
-        own_next().wait_send()
-        pass_next().wait_send()
-
-    @pl.when(parity == 1)
-    def _():
-        own_three().wait_send()
-        pass_back().wait_send()
+    for step in range(HEADS):
+        to_second(step).wait_send()
+
+        @pl.when(h != step)
+        def _():
+            pass_third(step).wait_send()
+
+        to_sibling(step).wait_send()
 
     for group in range(KV):
-        for delta in (1, 2, 3):
-            part_copy(group, delta).wait_send()
+        for which in range(2):
+            for piece in range(len(PIECES)):
+                part_copy(which, group, piece).wait_send()
 
 
 def shards(queries, key_states, value_states, out_grads, doc_blocks):
@@ -287,10 +318,10 @@
     out, dq, dk, dv = pl.pallas_call(
         kernel,
         out_shape=[
-            jax.ShapeDtypeStruct((SHARD, BLOCK, KV * QCOLS), bf16),
-            jax.ShapeDtypeStruct((SHARD, BLOCK, KV * QCOLS), bf16),
-            jax.ShapeDtypeStruct((tokens, KV * DH), bf16),
-            jax.ShapeDtypeStruct((tokens, KV * DH), bf16),
+            pltpu.VMEM((SHARD, BLOCK, KV * QCOLS), bf16),
+            pltpu.VMEM((SHARD, BLOCK, KV * QCOLS), bf16),
+            pltpu.VMEM((tokens, KV * DH), bf16),
+            pltpu.VMEM((tokens, KV * DH), bf16),
         ],
         in_specs=[pl.BlockSpec(memory_space=pltpu.SMEM)] + [anywhere] * 4,
         out_specs=[vmem] * 4,
@@ -298,20 +329,20 @@
             pltpu.VMEM((SHARD, BLOCK, KV * QCOLS), bf16),
             pltpu.VMEM((SHARD, BLOCK, KV * QCOLS), bf16),
             pltpu.VMEM((2, SLOTS * BLOCK, KV * DH), bf16),
-            pltpu.VMEM((KV, SLOTS * BLOCK, DH), f32),
-            pltpu.VMEM((KV, SLOTS * BLOCK, DH), f32),
-            pltpu.VMEM((2, KV, 12 * BLOCK, DH), bf16),
-            pltpu.VMEM((3, 2, KV, tokens, DH), bf16),
+            pltpu.VMEM((KV, DH, SLOTS * BLOCK), f32),
+            pltpu.VMEM((KV, DH, SLOTS * BLOCK), f32),
+            pltpu.VMEM((2, KV, DH, 12 * BLOCK), bf16),
+            pltpu.VMEM((2, KV, 3, DH, tokens), bf16),
             pltpu.VMEM((QCOLS, SPAN), bf16),
             pltpu.VMEM((QCOLS, SPAN), bf16),
             pltpu.VMEM((QCOLS, DH), bf16),
             dma((2, HEADS)), dma((2, HEADS)),
-            dma((4,)), dma((4,)),
+            dma((3, HEADS)), dma((3, HEADS)),
             dma((2, KV, HEADS)), dma((2, KV, HEADS)),
-            dma((KV, 3)), dma((KV, 3)),
+            dma((2, KV, 4)), dma((2, KV, 4)),
         ],
         compiler_params=pltpu.CompilerParams(
-            collective_id=0, has_side_effects=True, vmem_limit_bytes=60 * 2**20
+            collective_id=0, has_side_effects=True, vmem_limit_bytes=58 * 2**20
         ),
         name="attention",
     )(doc_blocks, queries, key_states, value_states, out_grads)

time: 111 us -> 89.8 us (0.81)
  the two profiles are of different devices: /device:TPU:6 before, /device:TPU:1 now
where the time goes in v2:
time: 89.8 us; the launch traced here: 89.7 us
  Pallas kernels  85 us (95%)
  local copies, waits for them, and re-layouts  4.04 us (4%)
    pallas_call x1, Pallas kernels, shards(): pl.pallas_call(kernel, out_shape=[pltpu.VMEM((SHARD, BLOCK, KV * QCOLS),...  85 us
    unnamed x4, local copies, waits for them, and re-layouts  4.04 us

profile of v2, /device:TPU:1, one launch (start us, length us, event | category | flops | bytes accessed | tf_op | source)
XLA Modules:
  0.0 89.7 jit_solution(1187112173972166454)
XLA Ops:
  0.6 85.0 %attention.1 = (bf16[4,128,2048]{2,1,0:T(8,128)(2,1)S(1)}, bf16[4,128,2048]{2,1,0:T(8,128)(2,1)S(1)}, bf16[512,256]{1,0:T(8,128)(2,1)S(1)}, bf16[512,256]{1,0:T(8,128)(2,1)S(1)}) custom-call(s32[16]{0:T(128)} %docs.1, bf16[128,8192]{1,0:T(8,128)(2,1)} %q_in.1, bf16[128,1024]{1,0:T(8,128)(2,1)} %k_in.1, bf16[128,1024]{1,0:T(8,128)(2,1)} %v_in.1, ...), custom_call_target="tpu_custom_call" | custom-call | tf_op jit(solution)/shard_map/attention/pallas_call | solution.py:318
  85.6 1.3 %copy.13 = bf16[512,2048]{1,0:T(8,128)(2,1)} copy(bf16[512,2048]{1,0:T(8,128)(2,1)S(1)} %bitcast.3) | data formatting | bytes 4194304
  87.0 1.3 %copy.14 = bf16[512,2048]{1,0:T(8,128)(2,1)} copy(bf16[512,2048]{1,0:T(8,128)(2,1)S(1)} %bitcast.2) | data formatting | bytes 4194304
  88.3 0.7 copy.15
  89.0 0.7 copy.16

commit v3 on v2

--- a/solution.py
+++ b/solution.py
@@ -199,7 +199,7 @@
         usual = 1 + lax.rem(2 * turn, 3)
         inner = (h * (3 - h)) // 2
         ending = (1 - inner) * (3 - turn) + inner * ((h - 1) * (1 + turn) + (2 - h) * usual)
-        step = (1 - early) * ((1 - group) * usual + group * ending)
+        step = (1 - early) * ending
         b = lax.rem(h + HEADS - step, HEADS)
         for which, buf in ((0, q_buf), (1, g_buf)):
             here = buf.at[b, :, columns(group * QCOLS, QCOLS)]
@@ -261,10 +261,15 @@
         dv_acc[group, :, window] += dot(gs_buf[...], p_buf[...], TN)
         dk_acc[group, :, window] += dot(q, ds_buf[...], TN)
 
+        @pl.when(index == HEADS - 1)
+        def _():
+            for which in (1, 0):
+                send_parts(which, 0, (0,))
+
         @pl.when(index == HEADS)
         def _():
             for which in (1, 0):
-                send_parts(which, 0, (0, 1, 2, 3))
+                send_parts(which, 0, (1, 2, 3))
 
         return 0
 

time: 89.8 us -> 89.4 us (level)
  no operation moved by 1% of the time
where the time goes in v3:
time: 89.4 us; the launch traced here: 89.3 us
  Pallas kernels  84.6 us (95%)
  local copies, waits for them, and re-layouts  4.04 us (5%)
    pallas_call x1, Pallas kernels, shards(): pl.pallas_call(kernel, out_shape=[pltpu.VMEM((SHARD, BLOCK, KV * QCOLS),...  84.6 us
    unnamed x4, local copies, waits for them, and re-layouts  4.04 us

profile of v3, /device:TPU:1, one launch (start us, length us, event | category | flops | bytes accessed | tf_op | source)
XLA Modules:
  0.0 89.3 jit_solution(3592871709872962444)
XLA Ops:
  0.6 84.6 %attention.1 = (bf16[4,128,2048]{2,1,0:T(8,128)(2,1)S(1)}, bf16[4,128,2048]{2,1,0:T(8,128)(2,1)S(1)}, bf16[512,256]{1,0:T(8,128)(2,1)S(1)}, bf16[512,256]{1,0:T(8,128)(2,1)S(1)}) custom-call(s32[16]{0:T(128)} %docs.1, bf16[128,8192]{1,0:T(8,128)(2,1)} %q_in.1, bf16[128,1024]{1,0:T(8,128)(2,1)} %k_in.1, bf16[128,1024]{1,0:T(8,128)(2,1)} %v_in.1, ...), custom_call_target="tpu_custom_call" | custom-call | tf_op jit(solution)/shard_map/attention/pallas_call | solution.py:323
  85.2 1.3 %copy.13 = bf16[512,2048]{1,0:T(8,128)(2,1)} copy(bf16[512,2048]{1,0:T(8,128)(2,1)S(1)} %bitcast.3) | data formatting | bytes 4194304
  86.5 1.3 %copy.14 = bf16[512,2048]{1,0:T(8,128)(2,1)} copy(bf16[512,2048]{1,0:T(8,128)(2,1)S(1)} %bitcast.2) | data formatting | bytes 4194304
  87.9 0.7 copy.15
  88.6 0.7 copy.16
